TPU v7x, 512 devices: a whole 4x8x8 slice. The times are simulated.
512 devices in a mesh: gx: 32 (over x, z), gy: 16 (over y, core).
Axes of the slice: x: 4, y: 8, z: 8, core: 2. Of those that a mesh axis runs over, the one named last changes fastest.
Arguments:
- source: float32 [512, 256, 256], P('gx', 'gy'), may hold values from -12 to 12
- inv_density: float32 [512, 256, 256], P('gx', 'gy'), may hold values from 0.4 to 2.5
Outputs:
- pressure: float32 [512, 256, 256], P('gx', 'gy')
All inputs are finite; a program needn't handle non-finite values.
Results may differ from a plain program's by a relative error of at most 0.0001.
Values sent between devices are 32-bit elements; how exact they have to be, the bound alone decides.
A program may use at most 128 MiB of HBM per device.

v0:
```python
import jax
import jax.numpy as jnp
from jax import lax
from jax.sharding import PartitionSpec as P

LEVELS = 4
NU_PRE = 2
NU_COARSE = 4
NU_POST = 2


aspect_ratio = 0.25


def with_halo(block, sides, width):
    for axis, dim in sides:
        count = lax.axis_size(axis)
        forward = [(i, i + 1) for i in range(count - 1)]
        forward.append((count - 1, 0))
        backward = [(target, source) for source, target in forward]
        low = lax.ppermute(
            lax.slice_in_dim(block, block.shape[dim] - width, None, axis=dim), axis, forward
        )
        high = lax.ppermute(lax.slice_in_dim(block, 0, width, axis=dim), axis, backward)
        block = jnp.concatenate([low, block, high], axis=dim)
    return block


def coefficients(beta_ext, weight):
    centre = beta_ext[1:-1, 1:-1]
    to_east = weight * 0.5 * (centre + beta_ext[2:, 1:-1])
    to_west = weight * 0.5 * (centre + beta_ext[:-2, 1:-1])
    to_north = weight * 0.5 * (centre + beta_ext[1:-1, 2:])
    to_south = weight * 0.5 * (centre + beta_ext[1:-1, :-2])
    upward = (
        aspect_ratio
        * 0.5
        * (centre + jnp.concatenate([centre[:, :, 1:], centre[:, :, -1:]], axis=2))
    )
    downward = (
        aspect_ratio
        * 0.5
        * (centre + jnp.concatenate([centre[:, :, :1], centre[:, :, :-1]], axis=2))
    )
    central = to_east + to_west + to_north + to_south + upward + downward
    return (to_east, to_west, to_north, to_south, upward, downward, central)


def neighbours(coeffs, extended):
    inner_part = extended[1:-1, 1:-1]
    zeros_layer = jnp.zeros_like(inner_part[:, :, :1])
    higher = jnp.concatenate([inner_part[:, :, 1:], zeros_layer], axis=2)
    beneath = jnp.concatenate([zeros_layer, inner_part[:, :, :-1]], axis=2)
    return (
        coeffs[0] * extended[2:, 1:-1]
        + coeffs[1] * extended[:-2, 1:-1]
        + coeffs[2] * extended[1:-1, 2:]
        + coeffs[3] * extended[1:-1, :-2]
        + coeffs[4] * higher
        + coeffs[5] * beneath
    )


def parity(shape):
    total = (
        lax.broadcasted_iota(jnp.int32, shape, 0)
        + lax.broadcasted_iota(jnp.int32, shape, 1)
        + lax.broadcasted_iota(jnp.int32, shape, 2)
    )
    return total % 2 == 0


def restrict(values):
    return values.reshape(values.shape[0] // 2, 2, values.shape[1] // 2, 2, values.shape[2]).mean(
        axis=(1, 3)
    )


def prolong(values):
    return jnp.repeat(jnp.repeat(values, 2, axis=0), 2, axis=1)


def rim_one(pressure):
    return with_halo(pressure, (("gx", 0), ("gy", 1)), 1)


def level_setup(beta, source, weight):
    narrow = coefficients(with_halo(beta, (("gx", 0), ("gy", 1)), 1), weight)
    return (narrow, narrow, source)


def smooth(pressure, source, setup, sweeps, from_zero):
    wide_coeffs, narrow, source_wide = setup
    red_cells = parity(pressure.shape)
    for sweep_index in range(sweeps):
        for colour_index, colour in enumerate((red_cells, jnp.logical_not(red_cells))):
            if from_zero and sweep_index == 0 and (colour_index == 0):
                extended = jnp.pad(pressure, ((1, 1), (1, 1), (0, 0)))
            else:
                extended = rim_one(pressure)
            pressure = jnp.where(
                colour, (source + neighbours(narrow, extended)) / narrow[6], pressure
            )
    return pressure


def on_device(source, inv_density):
    sources = [source]
    beta_levels = [inv_density]
    setups = []
    fields = []
    pressure = source
    for level_index in range(LEVELS):
        weight = 0.25**level_index
        sweeps = NU_COARSE if level_index == LEVELS - 1 else NU_PRE
        setup = level_setup(beta_levels[level_index], sources[level_index], weight)
        setups.append(setup)
        pressure = smooth(
            jnp.zeros_like(sources[level_index]), sources[level_index], setup, sweeps, True
        )
        if level_index < LEVELS - 1:
            fields.append(pressure)
            narrow = setup[1]
            leftover = sources[level_index] - (
                narrow[6] * pressure - neighbours(narrow, rim_one(pressure))
            )
            sources.append(restrict(leftover))
            beta_levels.append(restrict(beta_levels[level_index]))
    for level_index in range(LEVELS - 2, -1, -1):
        pressure = fields[level_index] + prolong(pressure)
        pressure = smooth(pressure, sources[level_index], setups[level_index], NU_POST, False)
    return pressure


def solution(mesh):
    placed = (P("gx", "gy", None), P("gx", "gy", None))
    return jax.shard_map(
        on_device, mesh=mesh, in_specs=placed, out_specs=P("gx", "gy", None), check_vma=False
    )
```

profile of v0, /device:TPU:1, one launch (start us, length us, event | category | flops | bytes accessed | tf_op | source)
XLA Modules:
  0.0 527.8 jit_solution(3216102616143894618)
XLA Ops:
  0.7 4.8 collective-permute-start.1
  5.6 10.8 %collective-permute-start = (f32[1,16,256]{2,1,0:T(8,128)S(1)}, f32[1,16,256]{2,1,0:T(8,128)S(1)}, u32[]{:S(2)}, u32[]{:S(2)}) collective-permute-start(f32[1,16,256]{2,1,0:T(8,128)S(1)} %get-tuple-element.82), channel_id=1, source_target_pairs={{16,0},{32,16},{48,32},{64,48},{80,64},{96,80},{112,96},{128,112},... | collective-permute-start | bytes 49160 | tf_op jit(solution)/shard_map/ppermute | solution.py:24
  23.2 6.7 %collective-permute-start.40 = (f32[1,4,256]{2,1,0:T(4,128)S(1)}, f32[1,4,256]{2,1,0:T(4,128)S(1)}, u32[]{:S(2)}, u32[]{:S(2)}) collective-permute-start(f32[1,4,256]{2,1,0:T(4,128)S(1)} %get-tuple-element.194), channel_id=1, source_target_pairs={{16,0},{32,16},{48,32},{64,48},{80,64},{96,80},{112,96},{128,112},... | collective-permute-start | bytes 12296 | tf_op jit(solution)/shard_map/ppermute | solution.py:24
  41.0 4.3 collective-permute-done.5
  45.3 4.7 collective-permute-start.6
  61.4 4.4 collective-permute-start.10
  72.7 4.4 collective-permute-done.13
  77.1 4.4 collective-permute-start.14
  84.7 6.7 %collective-permute-start.16 = (f32[1,16,256]{2,1,0:T(8,128)S(1)}, f32[1,16,256]{2,1,0:T(8,128)S(1)}, u32[]{:S(2)}, u32[]{:S(2)}) collective-permute-start(f32[1,16,256]{2,1,0:T(8,128)S(1)} %get-tuple-element.64), channel_id=1, source_target_pairs={{16,0},{32,16},{48,32},{64,48},{80,64},{96,80},{112,96},{128,112},... | collective-permute-start | bytes 49160 | tf_op jit(solution)/shard_map/ppermute | solution.py:24
  94.5 4.6 collective-permute-done.17
  110.4 5.2 collective-permute-start.60
  130.8 4.3 collective-permute-start.30
  146.1 4.3 collective-permute-start.34
  153.3 6.7 %collective-permute-start.36 = (f32[1,8,256]{2,1,0:T(8,128)S(1)}, f32[1,8,256]{2,1,0:T(8,128)S(1)}, u32[]{:S(2)}, u32[]{:S(2)}) collective-permute-start(f32[1,8,256]{2,1,0:T(8,128)S(1)} %get-tuple-element.120), channel_id=1, source_target_pairs={{16,0},{32,16},{48,32},{64,48},{80,64},{96,80},{112,96},{128,112},... | collective-permute-start | bytes 24584 | tf_op jit(solution)/shard_map/ppermute | solution.py:24
  163.1 4.6 collective-permute-done.37
  183.0 4.8 collective-permute-start.46
  240.1 4.9 collective-permute-done.65
  245.0 5.0 collective-permute-start.66
  408.1 4.3 collective-permute-done.109
  423.4 4.3 collective-permute-done.113
  427.7 4.3 collective-permute-start.114
  438.6 4.3 collective-permute-done.117
  443.0 4.3 collective-permute-start.118
  453.9 4.3 collective-permute-done.121
  458.3 4.3 collective-permute-start.122
  469.6 4.4 collective-permute-done.125
  485.2 4.4 collective-permute-done.129
  489.7 4.4 collective-permute-start.130
  500.9 4.4 collective-permute-done.133
  505.4 4.4 collective-permute-start.134
  516.7 4.4 collective-permute-done.137
  521.1 4.4 collective-permute-start.138
  (440 shorter events, 369.1 us)
Async XLA Ops:
  0.7 29.5 %collective-permute-start.1 = (f32[1,16,256]{2,1,0:T(8,128)S(1)}, f32[1,16,256]{2,1,0:T(8,128)S(1)}, u32[]{:S(2)}, u32[]{:S(2)}) collective-permute-start(f32[1,16,256]{2,1,0:T(8,128)S(1)} %get-tuple-element.81), channel_id=1, source_target_pairs={{0,16},{16,32},{32,48},{48,64},{64,80},{80,96},{96,112},{112,128},... | collective-permute-start | bytes 49160 | tf_op jit(solution)/shard_map/ppermute | solution.py:21
  5.6 24.7 %collective-permute-start = (f32[1,16,256]{2,1,0:T(8,128)S(1)}, f32[1,16,256]{2,1,0:T(8,128)S(1)}, u32[]{:S(2)}, u32[]{:S(2)}) collective-permute-start(f32[1,16,256]{2,1,0:T(8,128)S(1)} %get-tuple-element.82), channel_id=1, source_target_pairs={{16,0},{32,16},{48,32},{64,48},{80,64},{96,80},{112,96},{128,112},... | collective-permute-start | bytes 49160 | tf_op jit(solution)/shard_map/ppermute | solution.py:24
  17.7 73.7 %collective-permute-start.20 = (f32[1,8,256]{2,1,0:T(8,128)S(1)}, f32[1,8,256]{2,1,0:T(8,128)S(1)}, u32[]{:S(2)}, u32[]{:S(2)}) collective-permute-start(f32[1,8,256]{2,1,0:T(8,128)S(1)} %get-tuple-element.138), channel_id=1, source_target_pairs={{16,0},{32,16},{48,32},{64,48},{80,64},{96,80},{112,96},{128,112},... | collective-permute-start | bytes 24584 | tf_op jit(solution)/shard_map/ppermute | solution.py:24
  21.2 72.1 %collective-permute-start.21 = (f32[1,8,256]{2,1,0:T(8,128)S(1)}, f32[1,8,256]{2,1,0:T(8,128)S(1)}, u32[]{:S(2)}, u32[]{:S(2)}) collective-permute-start(f32[1,8,256]{2,1,0:T(8,128)S(1)} %get-tuple-element.137), channel_id=1, source_target_pairs={{0,16},{16,32},{32,48},{48,64},{64,80},{80,96},{96,112},{112,128},... | collective-permute-start | bytes 24584 | tf_op jit(solution)/shard_map/ppermute | solution.py:21
  23.2 136.8 %collective-permute-start.40 = (f32[1,4,256]{2,1,0:T(4,128)S(1)}, f32[1,4,256]{2,1,0:T(4,128)S(1)}, u32[]{:S(2)}, u32[]{:S(2)}) collective-permute-start(f32[1,4,256]{2,1,0:T(4,128)S(1)} %get-tuple-element.194), channel_id=1, source_target_pairs={{16,0},{32,16},{48,32},{64,48},{80,64},{96,80},{112,96},{128,112},... | collective-permute-start | bytes 12296 | tf_op jit(solution)/shard_map/ppermute | solution.py:24
  37.5 7.8 %collective-permute-start.5 = (f32[1,16,256]{2,1,0:T(8,128)S(1)}, f32[1,16,256]{2,1,0:T(8,128)S(1)}, u32[]{:S(2)}, u32[]{:S(2)}) collective-permute-start(f32[1,16,256]{2,1,0:T(8,128)S(1)} %get-tuple-element.75), channel_id=1, source_target_pairs={{0,16},{16,32},{32,48},{48,64},{64,80},{80,96},{96,112},{112,128},... | collective-permute-start | bytes 49160 | tf_op jit(solution)/shard_map/ppermute | solution.py:21
  53.6 7.8 %collective-permute-start.9 = (f32[1,16,256]{2,1,0:T(8,128)S(1)}, f32[1,16,256]{2,1,0:T(8,128)S(1)}, u32[]{:S(2)}, u32[]{:S(2)}) collective-permute-start(f32[1,16,256]{2,1,0:T(8,128)S(1)} %get-tuple-element.71), channel_id=1, source_target_pairs={{0,16},{16,32},{32,48},{48,64},{64,80},{80,96},{96,112},{112,128},... | collective-permute-start | bytes 49160 | tf_op jit(solution)/shard_map/ppermute | solution.py:21
  69.3 7.8 %collective-permute-start.13 = (f32[1,16,256]{2,1,0:T(8,128)S(1)}, f32[1,16,256]{2,1,0:T(8,128)S(1)}, u32[]{:S(2)}, u32[]{:S(2)}) collective-permute-start(f32[1,16,256]{2,1,0:T(8,128)S(1)} %get-tuple-element.67), channel_id=1, source_target_pairs={{0,16},{16,32},{32,48},{48,64},{64,80},{80,96},{96,112},{112,128},... | collective-permute-start | bytes 49160 | tf_op jit(solution)/shard_map/ppermute | solution.py:21
  82.4 79.6 %collective-permute-start.41 = (f32[1,4,256]{2,1,0:T(4,128)S(1)}, f32[1,4,256]{2,1,0:T(4,128)S(1)}, u32[]{:S(2)}, u32[]{:S(2)}) collective-permute-start(f32[1,4,256]{2,1,0:T(4,128)S(1)} %get-tuple-element.193), channel_id=1, source_target_pairs={{0,16},{16,32},{32,48},{48,64},{64,80},{80,96},{96,112},{112,128},... | collective-permute-start | bytes 12296 | tf_op jit(solution)/shard_map/ppermute | solution.py:21
  84.7 9.9 %collective-permute-start.16 = (f32[1,16,256]{2,1,0:T(8,128)S(1)}, f32[1,16,256]{2,1,0:T(8,128)S(1)}, u32[]{:S(2)}, u32[]{:S(2)}) collective-permute-start(f32[1,16,256]{2,1,0:T(8,128)S(1)} %get-tuple-element.64), channel_id=1, source_target_pairs={{16,0},{32,16},{48,32},{64,48},{80,64},{96,80},{112,96},{128,112},... | collective-permute-start | bytes 49160 | tf_op jit(solution)/shard_map/ppermute | solution.py:24
  91.4 7.8 %collective-permute-start.17 = (f32[1,16,256]{2,1,0:T(8,128)S(1)}, f32[1,16,256]{2,1,0:T(8,128)S(1)}, u32[]{:S(2)}, u32[]{:S(2)}) collective-permute-start(f32[1,16,256]{2,1,0:T(8,128)S(1)} %get-tuple-element.63), channel_id=1, source_target_pairs={{0,16},{16,32},{32,48},{48,64},{64,80},{80,96},{96,112},{112,128},... | collective-permute-start | bytes 49160 | tf_op jit(solution)/shard_map/ppermute | solution.py:21
  93.3 10.8 %collective-permute-start.22 = (f32[10,1,256]{2,1,0:T(1,128)S(1)}, f32[10,1,256]{2,1,0:T(1,128)S(1)}, u32[]{:S(2)}, u32[]{:S(2)}) collective-permute-start(f32[10,1,256]{2,1,0:T(1,128)S(1)} %get-tuple-element.100), channel_id=1, source_target_pairs={{1,0},{2,1},{3,2},{4,3},{5,4},{6,5},{7,6},{8,7},{9,8},{10,9},{11,1... | collective-permute-start | bytes 30728 | tf_op jit(solution)/shard_map/ppermute | solution.py:24
  105.1 10.6 %collective-permute-start.24 = (f32[1,8,256]{2,1,0:T(8,128)S(1)}, f32[1,8,256]{2,1,0:T(8,128)S(1)}, u32[]{:S(2)}, u32[]{:S(2)}) collective-permute-start(f32[1,8,256]{2,1,0:T(8,128)S(1)} %get-tuple-element.132), channel_id=1, source_target_pairs={{16,0},{32,16},{48,32},{64,48},{80,64},{96,80},{112,96},{128,112},... | collective-permute-start | bytes 24584 | tf_op jit(solution)/shard_map/ppermute | solution.py:24
  107.0 8.6 %collective-permute-start.25 = (f32[1,8,256]{2,1,0:T(8,128)S(1)}, f32[1,8,256]{2,1,0:T(8,128)S(1)}, u32[]{:S(2)}, u32[]{:S(2)}) collective-permute-start(f32[1,8,256]{2,1,0:T(8,128)S(1)} %get-tuple-element.131), channel_id=1, source_target_pairs={{0,16},{16,32},{32,48},{48,64},{64,80},{80,96},{96,112},{112,128},... | collective-permute-start | bytes 24584 | tf_op jit(solution)/shard_map/ppermute | solution.py:21
  110.4 99.2 %collective-permute-start.60 = (f32[1,2,256]{2,1,0:T(2,128)S(1)}, f32[1,2,256]{2,1,0:T(2,128)S(1)}, u32[]{:S(2)}, u32[]{:S(2)}) collective-permute-start(f32[1,2,256]{2,1,0:T(2,128)S(1)} %get-tuple-element.244), channel_id=1, source_target_pairs={{16,0},{32,16},{48,32},{64,48},{80,64},{96,80},{112,96},{128,112},... | collective-permute-start | bytes 6152 | tf_op jit(solution)/shard_map/ppermute | solution.py:24
  123.1 7.7 %collective-permute-start.29 = (f32[1,8,256]{2,1,0:T(8,128)S(1)}, f32[1,8,256]{2,1,0:T(8,128)S(1)}, u32[]{:S(2)}, u32[]{:S(2)}) collective-permute-start(f32[1,8,256]{2,1,0:T(8,128)S(1)} %get-tuple-element.127), channel_id=1, source_target_pairs={{0,16},{16,32},{32,48},{48,64},{64,80},{80,96},{96,112},{112,128},... | collective-permute-start | bytes 24584 | tf_op jit(solution)/shard_map/ppermute | solution.py:21
  138.4 7.7 %collective-permute-start.33 = (f32[1,8,256]{2,1,0:T(8,128)S(1)}, f32[1,8,256]{2,1,0:T(8,128)S(1)}, u32[]{:S(2)}, u32[]{:S(2)}) collective-permute-start(f32[1,8,256]{2,1,0:T(8,128)S(1)} %get-tuple-element.123), channel_id=1, source_target_pairs={{0,16},{16,32},{32,48},{48,64},{64,80},{80,96},{96,112},{112,128},... | collective-permute-start | bytes 24584 | tf_op jit(solution)/shard_map/ppermute | solution.py:21
  151.3 58.3 %collective-permute-start.61 = (f32[1,2,256]{2,1,0:T(2,128)S(1)}, f32[1,2,256]{2,1,0:T(2,128)S(1)}, u32[]{:S(2)}, u32[]{:S(2)}) collective-permute-start(f32[1,2,256]{2,1,0:T(2,128)S(1)} %get-tuple-element.243), channel_id=1, source_target_pairs={{0,16},{16,32},{32,48},{48,64},{64,80},{80,96},{96,112},{112,128},... | collective-permute-start | bytes 6152 | tf_op jit(solution)/shard_map/ppermute | solution.py:21
  153.3 9.8 %collective-permute-start.36 = (f32[1,8,256]{2,1,0:T(8,128)S(1)}, f32[1,8,256]{2,1,0:T(8,128)S(1)}, u32[]{:S(2)}, u32[]{:S(2)}) collective-permute-start(f32[1,8,256]{2,1,0:T(8,128)S(1)} %get-tuple-element.120), channel_id=1, source_target_pairs={{16,0},{32,16},{48,32},{64,48},{80,64},{96,80},{112,96},{128,112},... | collective-permute-start | bytes 24584 | tf_op jit(solution)/shard_map/ppermute | solution.py:24
  160.0 7.7 %collective-permute-start.37 = (f32[1,8,256]{2,1,0:T(8,128)S(1)}, f32[1,8,256]{2,1,0:T(8,128)S(1)}, u32[]{:S(2)}, u32[]{:S(2)}) collective-permute-start(f32[1,8,256]{2,1,0:T(8,128)S(1)} %get-tuple-element.119), channel_id=1, source_target_pairs={{0,16},{16,32},{32,48},{48,64},{64,80},{80,96},{96,112},{112,128},... | collective-permute-start | bytes 24584 | tf_op jit(solution)/shard_map/ppermute | solution.py:21
  162.0 10.1 %collective-permute-start.42 = (f32[6,1,256]{2,1,0:T(1,128)S(1)}, f32[6,1,256]{2,1,0:T(1,128)S(1)}, u32[]{:S(2)}, u32[]{:S(2)}) collective-permute-start(f32[6,1,256]{2,1,0:T(1,128)S(1)} %get-tuple-element.156), channel_id=1, source_target_pairs={{1,0},{2,1},{3,2},{4,3},{5,4},{6,5},{7,6},{8,7},{9,8},{10,9},{11,1... | collective-permute-start | bytes 18440 | tf_op jit(solution)/shard_map/ppermute | solution.py:24
  175.3 7.7 %collective-permute-start.45 = (f32[1,4,256]{2,1,0:T(4,128)S(1)}, f32[1,4,256]{2,1,0:T(4,128)S(1)}, u32[]{:S(2)}, u32[]{:S(2)}) collective-permute-start(f32[1,4,256]{2,1,0:T(4,128)S(1)} %get-tuple-element.187), channel_id=1, source_target_pairs={{0,16},{16,32},{32,48},{48,64},{64,80},{80,96},{96,112},{112,128},... | collective-permute-start | bytes 12296 | tf_op jit(solution)/shard_map/ppermute | solution.py:21
  219.4 9.0 %collective-permute-start.56 = (f32[1,4,256]{2,1,0:T(4,128)S(1)}, f32[1,4,256]{2,1,0:T(4,128)S(1)}, u32[]{:S(2)}, u32[]{:S(2)}) collective-permute-start(f32[1,4,256]{2,1,0:T(4,128)S(1)} %get-tuple-element.176), channel_id=1, source_target_pairs={{16,0},{32,16},{48,32},{64,48},{80,64},{96,80},{112,96},{128,112},... | collective-permute-start | bytes 12296 | tf_op jit(solution)/shard_map/ppermute | solution.py:24
  224.7 9.9 %collective-permute-start.62 = (f32[4,1,256]{2,1,0:T(1,128)S(1)}, f32[4,1,256]{2,1,0:T(1,128)S(1)}, u32[]{:S(2)}, u32[]{:S(2)}) collective-permute-start(f32[4,1,256]{2,1,0:T(1,128)S(1)} %get-tuple-element.210), channel_id=1, source_target_pairs={{1,0},{2,1},{3,2},{4,3},{5,4},{6,5},{7,6},{8,7},{9,8},{10,9},{11,1... | collective-permute-start | bytes 12296 | tf_op jit(solution)/shard_map/ppermute | solution.py:24
  404.7 7.7 %collective-permute-start.109 = (f32[1,8,256]{2,1,0:T(8,128)S(1)}, f32[1,8,256]{2,1,0:T(8,128)S(1)}, u32[]{:S(2)}, u32[]{:S(2)}) collective-permute-start(f32[1,8,256]{2,1,0:T(8,128)S(1)} %get-tuple-element.115), channel_id=1, source_target_pairs={{0,16},{16,32},{32,48},{48,64},{64,80},{80,96},{96,112},{112,128},... | collective-permute-start | bytes 24584 | tf_op jit(solution)/shard_map/ppermute | solution.py:21
  420.0 7.7 %collective-permute-start.113 = (f32[1,8,256]{2,1,0:T(8,128)S(1)}, f32[1,8,256]{2,1,0:T(8,128)S(1)}, u32[]{:S(2)}, u32[]{:S(2)}) collective-permute-start(f32[1,8,256]{2,1,0:T(8,128)S(1)} %get-tuple-element.111), channel_id=1, source_target_pairs={{0,16},{16,32},{32,48},{48,64},{64,80},{80,96},{96,112},{112,128},... | collective-permute-start | bytes 24584 | tf_op jit(solution)/shard_map/ppermute | solution.py:21
  435.3 7.7 %collective-permute-start.117 = (f32[1,8,256]{2,1,0:T(8,128)S(1)}, f32[1,8,256]{2,1,0:T(8,128)S(1)}, u32[]{:S(2)}, u32[]{:S(2)}) collective-permute-start(f32[1,8,256]{2,1,0:T(8,128)S(1)} %get-tuple-element.107), channel_id=1, source_target_pairs={{0,16},{16,32},{32,48},{48,64},{64,80},{80,96},{96,112},{112,128},... | collective-permute-start | bytes 24584 | tf_op jit(solution)/shard_map/ppermute | solution.py:21
  450.5 7.7 %collective-permute-start.121 = (f32[1,8,256]{2,1,0:T(8,128)S(1)}, f32[1,8,256]{2,1,0:T(8,128)S(1)}, u32[]{:S(2)}, u32[]{:S(2)}) collective-permute-start(f32[1,8,256]{2,1,0:T(8,128)S(1)} %get-tuple-element.103), channel_id=1, source_target_pairs={{0,16},{16,32},{32,48},{48,64},{64,80},{80,96},{96,112},{112,128},... | collective-permute-start | bytes 24584 | tf_op jit(solution)/shard_map/ppermute | solution.py:21
  466.2 7.8 %collective-permute-start.125 = (f32[1,16,256]{2,1,0:T(8,128)S(1)}, f32[1,16,256]{2,1,0:T(8,128)S(1)}, u32[]{:S(2)}, u32[]{:S(2)}) collective-permute-start(f32[1,16,256]{2,1,0:T(8,128)S(1)} %get-tuple-element.59), channel_id=1, source_target_pairs={{0,16},{16,32},{32,48},{48,64},{64,80},{80,96},{96,112},{112,128},... | collective-permute-start | bytes 49160 | tf_op jit(solution)/shard_map/ppermute | solution.py:21
  481.9 7.8 %collective-permute-start.129 = (f32[1,16,256]{2,1,0:T(8,128)S(1)}, f32[1,16,256]{2,1,0:T(8,128)S(1)}, u32[]{:S(2)}, u32[]{:S(2)}) collective-permute-start(f32[1,16,256]{2,1,0:T(8,128)S(1)} %get-tuple-element.55), channel_id=1, source_target_pairs={{0,16},{16,32},{32,48},{48,64},{64,80},{80,96},{96,112},{112,128},... | collective-permute-start | bytes 49160 | tf_op jit(solution)/shard_map/ppermute | solution.py:21
  497.6 7.8 %collective-permute-start.133 = (f32[1,16,256]{2,1,0:T(8,128)S(1)}, f32[1,16,256]{2,1,0:T(8,128)S(1)}, u32[]{:S(2)}, u32[]{:S(2)}) collective-permute-start(f32[1,16,256]{2,1,0:T(8,128)S(1)} %get-tuple-element.51), channel_id=1, source_target_pairs={{0,16},{16,32},{32,48},{48,64},{64,80},{80,96},{96,112},{112,128},... | collective-permute-start | bytes 49160 | tf_op jit(solution)/shard_map/ppermute | solution.py:21
  513.3 7.8 %collective-permute-start.137 = (f32[1,16,256]{2,1,0:T(8,128)S(1)}, f32[1,16,256]{2,1,0:T(8,128)S(1)}, u32[]{:S(2)}, u32[]{:S(2)}) collective-permute-start(f32[1,16,256]{2,1,0:T(8,128)S(1)} %get-tuple-element.47), channel_id=1, source_target_pairs={{0,16},{16,32},{32,48},{48,64},{64,80},{80,96},{96,112},{112,128},... | collective-permute-start | bytes 49160 | tf_op jit(solution)/shard_map/ppermute | solution.py:21
  (110 other events, 484.4 us)
where the time goes:
time: 531 us; the launch traced here: 528 us
  starting transfers between devices  348 us (66%)
  waiting for transfers between devices  164 us (31%)
  other arithmetic  7.51 us (1%)
  local copies, waits for them, and re-layouts  6.3 us (1%)
    ppermute x70, starting transfers between devices, with_halo(): lax.ppermute(lax.slice_in_dim(block, 0, width, axis=dim), axis, backward)  235 us
    ppermute x70, waiting for transfers between devices, with_halo(): lax.ppermute(lax.slice_in_dim(block, block.shape[dim] - width, None, axis...  140 us
    ppermute x70, starting transfers between devices, with_halo(): lax.ppermute(lax.slice_in_dim(block, block.shape[dim] - width, None, axis...  113 us
    ppermute x70, waiting for transfers between devices, with_halo(): lax.ppermute(lax.slice_in_dim(block, 0, width, axis=dim), axis, backward)  24.3 us
  transfers between devices with their start and end apart: 140, of which 93 were waited for; matrix products, arithmetic and copies ran while one was open for 2% of the time, Pallas kernels for 0%

commit v1 on v0

v1 whole, which is shorter than its diff:
```python
import jax
import jax.numpy as jnp
from jax import lax
from jax.experimental import pallas as pl
from jax.experimental.pallas import tpu as pltpu
from jax.sharding import PartitionSpec as P


MESH = pl.DeviceIdType.MESH
N = (16, 8, 4, 2)
HX = (6, 8, 8, 8)
HY = (6, 10, 10, 8)
XE = (28, 24, 20, 18)
YE = (32, 32, 32, 24)
WH = (0.5, 0.125, 0.03125, 0.0078125)
WV = 0.125
LANES = 128


def spread(n, radius, keep=None):
    out = []
    reach = -(-radius // n)
    for a in range(-reach, reach + 1):
        for b in range(-reach, reach + 1):
            gap_x = (abs(a) - 1) * n + 1 if a else 0
            gap_y = (abs(b) - 1) * n + 1 if b else 0
            if (a, b) == (0, 0) or gap_x + gap_y > radius:
                continue
            if keep is not None and not keep(a, b):
                continue
            rx, ry = radius - gap_y, radius - gap_x
            x0, x1 = max(-a * n, -rx), min(-a * n + n, n + rx)
            y0, y1 = max(-b * n, -ry), min(-b * n + n, n + ry)
            out.append((a, b, x0, x1 - x0, y0, y1 - y0))
    return out


def near(a, b):
    return max(abs(a), abs(b)) == 1


def far(a, b):
    return max(abs(a), abs(b)) > 1


GROUPS = {
    "b0": (0, 2, spread(16, 4)),
    "e0": (0, 2, spread(16, 5)),
    "e1": (1, 2, spread(8, 7)),
    "e2": (2, 2, spread(4, 8)),
    "e3": (3, 2, spread(2, 7)),
    "f0": (0, 1, spread(16, 4)),
    "b1": (1, 2, spread(8, 6)),
    "f1": (1, 1, spread(8, 7)),
    "b2": (2, 2, spread(4, 8, near)),
    "b2far": (2, 2, spread(4, 7, far)),
    "f2": (2, 1, spread(4, 8)),
    "b3": (3, 2, spread(2, 6)),
    "f3": (3, 1, spread(2, 6)),
}
NAMES = tuple(GROUPS)
COUNT = {k: c * sum(m[3] * m[5] for m in msgs) for k, (_, c, msgs) in GROUPS.items()}
MOST = -(-max(COUNT.values()) // 8) * 8
PARTNERS = sorted({m[:2] for _, _, msgs in GROUPS.values() for m in msgs})


def rows(x0, nx, body, group=4):
    steps = nx // group
    if steps > 1:

        def step(i, carry):
            for j in range(group):
                body(x0 + i * group + j, (x0 + j) % 2)
            return carry

        lax.fori_loop(0, steps, step, 0)
        done = steps * group
    else:
        done = 0
    for j in range(done, nx):
        body(x0 + j, (x0 + j) % 2)


def odd_rows(n, offset):
    return (lax.broadcasted_iota(jnp.int32, (n, LANES), 0) + offset) % 2 == 1


def kernel(gx_size, gy_size, src_ref, inv_ref, out_ref, *scratch):
    (e0, e1, e2, e3, b0, b1, b2, b3, p0, p1, p2, p3, q0, q1, q2, q3, d0, d1, d2, d3,
     g0, g1, g2, f0, f1, f2, f3, b2w, res, dummy, send_sem, recv_sem) = scratch
    beta, b, p, q, inv = (e0, e1, e2, e3), (b0, b1, b2, b3), (p0, p1, p2, p3), (q0, q1, q2, q3), (d0, d1, d2, d3)
    diag, field = (g0, g1, g2), (f0, f1, f2, f3)
    sent = {"b0": b0, "e0": e0, "e1": e1, "e2": e2, "e3": e3, "f0": f0, "b1": b1, "f1": f1,
            "b2": b2, "b2far": b2, "f2": f2, "b3": b3, "f3": f3}
    landed = dict(sent, b2far=b2w)

    ix, iy = lax.axis_index("gx"), lax.axis_index("gy")
    at_x = {a: lax.rem(ix + (a + gx_size), gx_size) for a in range(-4, 5)}
    at_y = {a: lax.rem(iy + (a + gy_size), gy_size) for a in range(-4, 5)}

    def device(a, c):
        return {"gx": at_x[a], "gy": at_y[c]}

    def send(name):
        level, colours, msgs = GROUPS[name]
        k, n = NAMES.index(name), N[level]
        for a, c, x0, nx, y0, ny in msgs:
            here = (pl.ds(HX[level] + x0 + a * n, nx), pl.ds(HY[level] + y0 + c * n, ny))
            there = (pl.ds(HX[level] + x0, nx), pl.ds(HY[level] + y0, ny))
            if colours == 2:
                here, there = (slice(None),) + here, (slice(None),) + there
            pltpu.make_async_remote_copy(
                src_ref=sent[name].at[here], dst_ref=landed[name].at[there],
                send_sem=send_sem.at[k], recv_sem=recv_sem.at[k],
                device_id=device(a, c), device_id_type=MESH,
            ).start()

    def await_bytes(sem, name):
        block = dummy.at[pl.ds(0, COUNT[name])]
        pltpu.make_async_copy(block, block, sem.at[NAMES.index(name)]).wait()

    def receive(*names):
        for name in names:
            await_bytes(recv_sem, name)

    lane = lax.broadcasted_iota(jnp.int32, (8, LANES), 1)
    odd8 = odd_rows(8, 0)

    def weights(kind):
        down = jnp.logical_not(odd8) if kind == 0 else odd8
        first = jnp.where(jnp.logical_and(down, lane > 0), 1.0, 0.0)
        second = jnp.where(jnp.logical_and(jnp.logical_not(down), lane < LANES - 1), 1.0, 0.0)
        return first[None], second[None], (1.0 - first - second)[None]

    weight = (weights(0), weights(1))

    def load(ref, lead, y0, n):
        return ref[lead + (pl.ds(y0, n),)].reshape(n // 8, 8, LANES)

    def store(ref, lead, y0, n, value):
        ref[lead + (pl.ds(y0, n),)] = value.reshape(n, LANES)

    def beside(same, kind):
        flat = same.reshape(-1, LANES)
        lower = pltpu.roll(flat, 1, 1).reshape(same.shape)
        upper = pltpu.roll(flat, LANES - 1, 1).reshape(same.shape)
        return lower * weight[kind][0] + upper * weight[kind][1]

    def around(ref, other, x, y0, n):
        return (load(ref, (other, x - 1), y0, n) + load(ref, (other, x + 1), y0, n)) + (
            load(ref, (other, x), y0 - 1, n) + load(ref, (other, x), y0 + 1, n))

    def set_up(level, x0, nx, y0, n):
        wh = WH[level]

        def body(x, px):
            for c in (0, 1):
                kind = (c + px) % 2
                centre = load(beta[level], (c, x), y0, n)
                same = load(beta[level], (1 - c, x), y0, n)
                vertical = same + beside(same, kind) + centre * weight[kind][2]
                total = centre * (4 * wh + 2 * WV) + wh * around(beta[level], 1 - c, x, y0, n) + WV * vertical
                store(inv[level], (c, x), y0, n, 1.0 / total)
                if c == 0 and level < 3:
                    store(diag[level], (x,), y0, n, total)

        rows(x0, nx, body, 2)

    def coupled(level, c, x, px, y0, n):
        wh, kind = WH[level], (c + px) % 2
        same_p, same_q = load(p[level], (1 - c, x), y0, n), load(q[level], (1 - c, x), y0, n)
        sum_p = wh * around(p[level], 1 - c, x, y0, n) + WV * (same_p + beside(same_p, kind))
        sum_q = wh * around(q[level], 1 - c, x, y0, n) + WV * (same_q + beside(same_q, kind))
        centre = load(beta[level], (c, x), y0, n)
        return centre, centre * sum_p + sum_q

    def half_sweep(level, c, radius, y0, n, rhs=None):
        rhs = b[level] if rhs is None else rhs

        def body(x, px):
            centre, total = coupled(level, c, x, px, y0, n)
            value = (load(rhs, (c, x), y0, n) + total) * load(inv[level], (c, x), y0, n)
            store(p[level], (c, x), y0, n, value)
            store(q[level], (c, x), y0, n, centre * value)

        rows(HX[level] - radius, N[level] + 2 * radius, body)

    def first_half(level, radius, y0, n):
        def body(x, px):
            value = load(b[level], (0, x), y0, n) * load(inv[level], (0, x), y0, n)
            store(p[level], (0, x), y0, n, value)
            store(q[level], (0, x), y0, n, load(beta[level], (0, x), y0, n) * value)

        rows(HX[level] - radius, N[level] + 2 * radius, body)

    def put_coarse(ref, level, i, even, odd):
        n = N[level]

        def put(parity):
            swapped = odd_rows(n, parity)
            here = (HX[level] + i, pl.ds(HY[level], n))
            ref[(0,) + here] = jnp.where(swapped, odd, even)
            ref[(1,) + here] = jnp.where(swapped, even, odd)

        return put

    def coarsen_beta(level):
        n = N[level + 1]

        def body(i, pi):
            def child(c, a, k):
                return beta[level][c, HX[level] + 2 * i + a, pl.ds(HY[level] + k, n, stride=2), :]

            even = 0.25 * ((child(0, 0, 0) + child(0, 1, 1)) + (child(1, 0, 1) + child(1, 1, 0)))
            odd = 0.25 * ((child(1, 0, 0) + child(1, 1, 1)) + (child(0, 0, 1) + child(0, 1, 0)))
            put_coarse(beta[level + 1], level + 1, i, even, odd)(pi)

        rows(0, n, body)

    def residual(level):
        n, nc = N[level], N[level + 1]
        padded = max(8, n)

        def body(x, px):
            _, total = coupled(level, 0, x, px, HY[level], padded)
            left = load(b[level], (0, x), HY[level], padded) + total
            left = left - load(diag[level], (x,), HY[level], padded) * load(p[level], (0, x), HY[level], padded)
            store(res, (x - HX[level],), 0, padded, left)
            field[level][x, pl.ds(HY[level], n)] = p[level][1, x, pl.ds(HY[level], n)]

        rows(HX[level], n, body)

        def restrict(i, pi):
            def child(a, k):
                return res[2 * i + a, pl.ds(k, nc, stride=2), :]

            put_coarse(b[level + 1], level + 1, i, 0.25 * (child(0, 0) + child(1, 1)), 0.25 * (child(0, 1) + child(1, 0)))(pi)

        rows(0, nc, restrict)

    def prolong(level, x0, nx, y0, n):
        half = n // 2
        i0 = HX[level + 1] + (x0 - HX[level]) // 2
        j0 = HY[level + 1] + (y0 - HY[level]) // 2

        def body(i, pi):
            red = p[level + 1][0, i, pl.ds(j0, half), :]
            black = p[level + 1][1, i, pl.ds(j0, half), :]
            swapped = odd_rows(half, j0 + pi)
            even, odd = jnp.where(swapped, black, red), jnp.where(swapped, red, black)
            for a in (0, 1):
                x = x0 + 2 * (i - i0) + a
                for k in (0, 1):
                    here = (pl.ds(y0 + k, half, stride=2), slice(None))
                    value = field[level][(x,) + here] + (odd if a == k else even)
                    p[level][(1, x) + here] = value
                    q[level][(1, x) + here] = beta[level][(1, x) + here] * value

        rows(i0, nx // 2, body, 2)

    def descend(level, y0, n):
        first_half(level, 4, y0, n)
        half_sweep(level, 1, 3, y0, n)
        half_sweep(level, 0, 2, y0, n)
        half_sweep(level, 1, 1, y0, n)
        residual(level)

    barrier = pltpu.get_barrier_semaphore()
    for a, c in PARTNERS:
        pl.semaphore_signal(barrier, inc=1, device_id=device(a, c), device_id_type=MESH)

    wide = lax.broadcasted_iota(jnp.int32, (16, LANES), 1)

    def take(x, px):
        odd = odd_rows(16, px).astype(jnp.int32)
        low = wide < LANES // 2
        for ref, to in ((inv_ref, e0), (src_ref, b0)):
            lower, upper = ref[x, :, pl.ds(0, LANES)], ref[x, :, pl.ds(LANES, LANES)]
            for c in (0, 1):
                slot = lax.rem(2 * wide + (odd if c == 0 else 1 - odd), LANES)
                value = jnp.where(low, jnp.take_along_axis(lower, slot, axis=1), jnp.take_along_axis(upper, slot, axis=1))
                to[c, HX[0] + x, pl.ds(HY[0], 16)] = value

    rows(0, 16, take)
    pl.semaphore_wait(barrier, len(PARTNERS))
    send("e0")
    send("b0")
    for level in (0, 1, 2):
        coarsen_beta(level)
    send("e1")
    receive("e0")
    receive("b0")
    set_up(0, 2, 24, 2, 24)
    descend(0, 2, 24)

    send("b1")
    send("f0")
    send("e2")
    receive("e1")
    set_up(1, 2, 20, 2, 24)
    receive("b1")
    descend(1, 6, 16)

    send("b2")
    send("f1")
    send("e3")
    receive("e2")
    set_up(2, 1, 18, 2, 24)
    receive("b2")
    descend(2, 6, 16)

    send("b3")
    send("b2far")
    send("f2")
    receive("e3")
    set_up(3, 2, 14, 2, 16)
    receive("b3")
    first_half(3, 6, 2, 16)
    for step in range(1, 7):
        half_sweep(3, step % 2, 6 - step, 2, 16)
    for x in range(HX[3], HX[3] + N[3]):
        f3[x, pl.ds(HY[3], N[3])] = p3[0, x, pl.ds(HY[3], N[3])]
    send("f3")

    def keep_rhs(x, px):
        for c in (0, 1):
            b2w[c, x, pl.ds(6, 12)] = b2[c, x, pl.ds(6, 12)]

    rows(4, 12, keep_rhs)
    for name in NAMES:
        if name != "f3":
            await_bytes(send_sem, name)
    receive("f3")

    def red_back(x, px):
        value = load(f3, (x,), 2, 16)
        store(p3, (0, x), 2, 16, value)
        store(q3, (0, x), 2, 16, load(e3, (0, x), 2, 16) * value)

    rows(2, 14, red_back)
    half_sweep(3, 1, 5, 2, 16)

    receive("b2far")
    receive("f2")
    prolong(2, 0, 20, 2, 24)
    for step in range(4):
        half_sweep(2, step % 2, 7 - step, 2, 24, b2w)
    receive("f1")
    prolong(1, 0, 24, 2, 24)
    for step in range(4):
        half_sweep(1, step % 2, 6 - step, 2, 24)
    receive("f0")
    prolong(0, 2, 24, 2, 24)
    half_sweep(0, 0, 3, 2, 24)
    half_sweep(0, 1, 2, 2, 24)
    half_sweep(0, 0, 1, 2, 24)
    half_sweep(0, 1, 0, 6, 16)

    def give(x, px):
        red, black = p0[0, HX[0] + x, pl.ds(HY[0], 16)], p0[1, HX[0] + x, pl.ds(HY[0], 16)]
        is_red = (wide + odd_rows(16, px).astype(jnp.int32)) % 2 == 0
        for part in (0, 1):
            slot = wide // 2 + part * (LANES // 2)
            out_ref[x, :, pl.ds(part * LANES, LANES)] = jnp.where(
                is_red, jnp.take_along_axis(red, slot, axis=1), jnp.take_along_axis(black, slot, axis=1))

    rows(0, 16, give)
    await_bytes(send_sem, "f3")


def solution(mesh):
    gx_size, gy_size = mesh.shape["gx"], mesh.shape["gy"]

    def both(level):
        return pltpu.VMEM((2, XE[level], YE[level], LANES), jnp.float32)

    def single(level):
        return pltpu.VMEM((XE[level], YE[level], LANES), jnp.float32)

    levels = range(4)
    scratch = [both(level) for _ in range(5) for level in levels]
    scratch += [single(level) for level in range(3)] + [single(level) for level in levels]
    scratch += [both(2), pltpu.VMEM((16, 16, LANES), jnp.float32), pltpu.VMEM((MOST, LANES), jnp.float32)]
    scratch += [pltpu.SemaphoreType.DMA((len(NAMES),))] * 2

    def on_device(source, inv_density):
        vmem = pl.BlockSpec(memory_space=pltpu.VMEM)

        def body(*refs):
            kernel(gx_size, gy_size, *refs)

        return pl.pallas_call(
            body,
            out_shape=jax.ShapeDtypeStruct(source.shape, jnp.float32),
            in_specs=[vmem, vmem],
            out_specs=vmem,
            scratch_shapes=scratch,
            name="v_cycle",
            compiler_params=pltpu.CompilerParams(
                collective_id=0, has_side_effects=True, vmem_limit_bytes=40 << 20
            ),
        )(source, inv_density)

    placed = P("gx", "gy", None)
    return jax.shard_map(
        on_device, mesh=mesh, in_specs=(placed, placed), out_specs=placed, check_vma=False
    )
```

time: 531 us -> 66.8 us (0.13)
  starting transfers between devices: 348 us -> 0 us
  waiting for transfers between devices: 164 us -> 0 us
  Pallas kernels: 0 us -> 64 us
  other arithmetic: 7.51 us -> 0 us
    ppermute x140 -> x0, starting transfers between devices: 348 us -> none  [the longest x70 235 us: with_halo(): lax.ppermute(lax.slice_in_dim(block, 0, width, axis=dim), axis, backward)]
    ppermute x140 -> x0, waiting for transfers between devices: 164 us -> none  [the longest x70 140 us: with_halo(): lax.ppermute(lax.slice_in_dim(block, block.shape[dim] - width, None, axis...]
    pallas_call x0 -> x1, Pallas kernels: none -> 64 us  [on_device(): pl.pallas_call(body, out_shape=jax.ShapeDtypeStruct(source.shape, jnp.flo...]
    select_n x32 -> x0, other arithmetic: 5.88 us -> none  [smooth(): jnp.where(colour, (source + neighbours(narrow, extended)) / narrow[6], pr...]
  transfers between devices with their start and end apart: 140 -> 0, of which waited for: 93 -> 0; matrix products, arithmetic and copies ran while one was open for 2% -> 0% of each run, Pallas kernels for 0% -> 0%
where the time goes in v1:
time: 66.8 us; the launch traced here: 66.6 us
  Pallas kernels  64 us (96%)
  local copies, waits for them, and re-layouts  2.6 us (4%)
    pallas_call x1, Pallas kernels, on_device(): pl.pallas_call(body, out_shape=jax.ShapeDtypeStruct(source.shape, jnp.flo...  64 us
    unnamed x5, local copies, waits for them, and re-layouts  2.6 us

profile of v1, /device:TPU:1, one launch (start us, length us, event | category | flops | bytes accessed | tf_op | source)
XLA Modules:
  0.0 66.6 jit_solution(8885006569703780845)
XLA Ops:
  0.0 0.0 copy-start
  0.0 0.9 %copy-done = f32[16,16,256]{2,1,0:T(8,128)S(1)} copy-done((f32[16,16,256]{2,1,0:T(8,128)S(1)}, f32[16,16,256]{2,1,0:T(8,128)}, u32[]{:S(2)}) %copy-start) | copy-done | bytes 262168
  1.0 0.0 copy-start.1
  1.0 0.9 %copy-done.1 = f32[16,16,256]{2,1,0:T(8,128)S(1)} copy-done((f32[16,16,256]{2,1,0:T(8,128)S(1)}, f32[16,16,256]{2,1,0:T(8,128)}, u32[]{:S(2)}) %copy-start.1) | copy-done | bytes 262168
  1.9 64.0 %v_cycle.1 = f32[16,16,256]{2,1,0:T(8,128)S(1)} custom-call(f32[16,16,256]{2,1,0:T(8,128)S(1)} %copy-done, f32[16,16,256]{2,1,0:T(8,128)S(1)} %copy-done.1), custom_call_target="tpu_custom_call" | custom-call | tf_op jit(solution)/shard_map/v_cycle/pallas_call | solution.py:392
  65.9 0.7 %copy.4 = f32[16,16,256]{2,1,0:T(8,128)} copy(f32[16,16,256]{2,1,0:T(8,128)S(1)} %v_cycle.1) | data formatting | bytes 524288
Async XLA Ops:
  0.0 0.9 %copy-start = (f32[16,16,256]{2,1,0:T(8,128)S(1)}, f32[16,16,256]{2,1,0:T(8,128)}, u32[]{:S(2)}) copy-start(f32[16,16,256]{2,1,0:T(8,128)} %refs_0_.1) | copy-start | bytes 786436
  1.0 0.9 %copy-start.1 = (f32[16,16,256]{2,1,0:T(8,128)S(1)}, f32[16,16,256]{2,1,0:T(8,128)}, u32[]{:S(2)}) copy-start(f32[16,16,256]{2,1,0:T(8,128)} %refs_1_.1) | copy-start | bytes 786436

commit v2 on v1

v2 whole, which is shorter than its diff:
```python
import jax
import jax.numpy as jnp
from jax import lax
from jax.experimental import pallas as pl
from jax.experimental.pallas import tpu as pltpu
from jax.sharding import PartitionSpec as P


MESH = pl.DeviceIdType.MESH
N = (16, 8, 4, 2)
HX = (6, 8, 8, 8)
HY = (6, 10, 10, 8)
XE = (28, 24, 20, 18)
YE = (32, 32, 32, 24)
WH = (0.5, 0.125, 0.03125, 0.0078125)
WV = 0.125
LANES = 128
GROUP = 24


def spread(n, radius, keep=None):
    out = []
    reach = -(-radius // n)
    for a in range(-reach, reach + 1):
        for b in range(-reach, reach + 1):
            gap_x = (abs(a) - 1) * n + 1 if a else 0
            gap_y = (abs(b) - 1) * n + 1 if b else 0
            if (a, b) == (0, 0) or gap_x + gap_y > radius:
                continue
            if keep is not None and not keep(a, b):
                continue
            rx, ry = radius - gap_y, radius - gap_x
            x0, x1 = max(-a * n, -rx), min(-a * n + n, n + rx)
            y0, y1 = max(-b * n, -ry), min(-b * n + n, n + ry)
            out.append((a, b, x0, x1 - x0, y0, y1 - y0))
    return sorted(out, key=lambda m: (m[1] != 0, m[0] == 0))


def near(a, b):
    return max(abs(a), abs(b)) == 1


def far(a, b):
    return max(abs(a), abs(b)) > 1


BOTH, ONE, RED, BLACK = (slice(None),), (), (0,), (1,)
GROUPS = {
    "b0": (0, RED, spread(16, 4)),
    "b0k": (0, BLACK, spread(16, 3)),
    "e0": (0, RED, spread(16, 4)),
    "e0k": (0, BLACK, spread(16, 5)),
    "e1": (1, BOTH, spread(8, 7)),
    "e2": (2, BOTH, spread(4, 8)),
    "e3": (3, BOTH, spread(2, 7)),
    "f0": (0, ONE, spread(16, 4)),
    "b1": (1, BOTH, spread(8, 6)),
    "f1": (1, ONE, spread(8, 7)),
    "b2": (2, BOTH, spread(4, 8, near)),
    "b2far": (2, BOTH, spread(4, 7, far)),
    "f2": (2, ONE, spread(4, 8)),
    "b3": (3, BOTH, spread(2, 6)),
    "f3": (3, ONE, spread(2, 6)),
}
NAMES = tuple(GROUPS)
COUNT = {k: (2 if c == BOTH else 1) * sum(m[3] * m[5] for m in msgs) for k, (_, c, msgs) in GROUPS.items()}
MOST = -(-max(COUNT.values()) // 8) * 8
PARTNERS = [m[:2] for m in GROUPS["e2"][2]]


def rows(x0, nx, body, group=4):
    steps = nx // group
    if steps > 1:

        def step(i, carry):
            for j in range(group):
                body(x0 + i * group + j, (x0 + j) % 2)
            return carry

        lax.fori_loop(0, steps, step, 0)
        done = steps * group
    else:
        done = 0
    for j in range(done, nx):
        body(x0 + j, (x0 + j) % 2)


def odd_rows(n, offset):
    return (lax.broadcasted_iota(jnp.int32, (n, LANES), 0) + offset) % 2 == 1


def lines(level, radius):
    return HY[level] - radius, -(-(N[level] + 2 * radius) // 8) * 8


def kernel(gx_size, gy_size, src_hbm, inv_hbm, out_ref, *scratch):
    beta, b, norm, red_p, black_p, coef = (scratch[4 * k : 4 * k + 4] for k in range(6))
    diag, field = scratch[24:27], scratch[27:31]
    b2w, res, src_ref, inv_ref, dummy, load_sem, send_sem, recv_sem = scratch[31:]
    sent = {"b2far": b[2], "b0k": b[0], "e0k": beta[0]}
    for level in range(4):
        sent.update({"e%d" % level: beta[level], "b%d" % level: b[level], "f%d" % level: field[level]})
    landed = dict(sent, b2far=b2w)

    ix, iy = lax.axis_index("gx"), lax.axis_index("gy")
    at_x = {a: lax.rem(ix + (a + gx_size), gx_size) for a in range(-4, 5)}
    at_y = {a: lax.rem(iy + (a + gy_size), gy_size) for a in range(-4, 5)}

    def device(a, c):
        return {"gx": at_x[a], "gy": at_y[c]}

    def send(name):
        level, colours, msgs = GROUPS[name]
        k, n = NAMES.index(name), N[level]
        for a, c, x0, nx, y0, ny in msgs:
            here = (pl.ds(HX[level] + x0 + a * n, nx), pl.ds(HY[level] + y0 + c * n, ny))
            there = (pl.ds(HX[level] + x0, nx), pl.ds(HY[level] + y0, ny))
            here, there = colours + here, colours + there
            pltpu.make_async_remote_copy(
                src_ref=sent[name].at[here], dst_ref=landed[name].at[there],
                send_sem=send_sem.at[k], recv_sem=recv_sem.at[k],
                device_id=device(a, c), device_id_type=MESH,
            ).start()

    def await_bytes(sem, name):
        block = dummy.at[pl.ds(0, COUNT[name])]
        pltpu.make_async_copy(block, block, sem.at[NAMES.index(name)]).wait()

    def receive(*names):
        for name in names:
            await_bytes(recv_sem, name)

    lane = lax.broadcasted_iota(jnp.int32, (8, LANES), 1)
    odd8 = odd_rows(8, 0)

    def weights(kind):
        down = jnp.logical_not(odd8) if kind == 0 else odd8
        has = jnp.where(down, jnp.where(lane > 0, 1.0, 0.0), jnp.where(lane < LANES - 1, 1.0, 0.0))
        return jnp.where(down, 1.0, 0.0)[None], has[None]

    weight = (weights(0), weights(1))

    def load(ref, lead, y0, n):
        return ref[lead + (pl.ds(y0, n),)].reshape(n // 8, 8, LANES)

    def store(ref, lead, y0, n, value):
        ref[lead + (pl.ds(y0, n),)] = value.reshape(n, LANES)

    def beside(same, kind):
        flat = same.reshape(-1, LANES)
        lower = pltpu.roll(flat, 1, 1).reshape(same.shape)
        upper = pltpu.roll(flat, LANES - 1, 1).reshape(same.shape)
        return jnp.where(weight[kind][0] > 0.0, lower, upper)

    def set_up(level, radius, group):
        wh = WH[level]
        y0, n = lines(level, radius)

        def body(x, px):
            for c in (0, 1):
                kind = (c + px + y0) % 2
                at = lambda dx, dy: load(beta[level], (1 - c, x + dx), y0 + dy, n)
                centre, same = load(beta[level], (c, x), y0, n), at(0, 0)
                has = weight[kind][1]
                other = beside(same, kind)
                other = other * has + centre * (1.0 - has)
                sides = (at(1, 0), at(-1, 0), at(0, 1), at(0, -1))
                total = centre * (4 * wh + 2 * WV) + wh * ((sides[0] + sides[1]) + (sides[2] + sides[3])) + WV * (same + other)
                inverse = 1.0 / total
                across, upright = wh * inverse, WV * inverse
                for k, side in enumerate(sides):
                    store(coef[level], (k, c, x), y0, n, (centre + side) * across)
                store(coef[level], (4, c, x), y0, n, (centre + same) * upright)
                store(coef[level], (5, c, x), y0, n, (centre + other) * (upright * has))
                store(coef[level], (6, c, x), y0, n, inverse)
                if c == 0 and level < 3:
                    store(diag[level], (x,), y0, n, total)

        rows(HX[level] - radius, N[level] + 2 * radius, body, group)

    def normalise(level, radius, rhs=None):
        y0, n = lines(level, radius)
        rhs = b[level] if rhs is None else rhs

        def body(x, px):
            for c in (0, 1):
                store(norm[level], (c, x), y0, n, load(rhs, (c, x), y0, n) * load(coef[level], (6, c, x), y0, n))

        rows(HX[level] - radius, N[level] + 2 * radius, body, 10)

    def solved(level, c, x0, count, y0, n, other, lead=()):
        mids = [load(other, lead + (x0 + j - 1,), y0, n) for j in range(count + 2)]
        out = []
        for j in range(count):
            x = x0 + j
            kind = (c + j + y0) % 2
            factor = lambda k: load(coef[level], (k, c, x), y0, n)
            value = load(norm[level], (c, x), y0, n) + mids[j + 2] * factor(0)
            value2 = mids[j] * factor(1) + load(other, lead + (x,), y0 + 1, n) * factor(2)
            value3 = load(other, lead + (x,), y0 - 1, n) * factor(3) + mids[j + 1] * factor(4)
            out.append((kind, mids[j + 1], factor(5), (value + value2) + value3))
        return out

    def finish(out, px):
        return [total + beside(same, (kind + px) % 2) * factor for kind, same, factor, total in out]

    def chunks(x0, count, body, group):
        steps = count // group
        if steps > 1:

            def step(i, carry):
                body(x0 + i * group, x0 % 2, group)
                return carry

            lax.fori_loop(0, steps, step, 0)
            left = count - steps * group
        else:
            left = count
        if left:
            body(x0 + count - left, (x0 + count - left) % 2, left)

    def half_sweep(level, c, radius, other=None, lead=(), group=GROUP):
        y0, n = lines(level, radius)
        mine = (red_p, black_p)[c][level]
        other = (black_p, red_p)[c][level] if other is None else other

        def body(x, px, count):
            values = finish(solved(level, c, x, count, y0, n, other, lead), px)
            for j, value in enumerate(values):
                store(mine, (x + j,), y0, n, value)

        chunks(HX[level] - radius, N[level] + 2 * radius, body, group)

    def put_coarse(ref, level, i, even, odd):
        n = N[level]

        def put(parity):
            swapped = odd_rows(n, parity)
            here = (HX[level] + i, pl.ds(HY[level], n))
            ref[(0,) + here] = jnp.where(swapped, odd, even)
            ref[(1,) + here] = jnp.where(swapped, even, odd)

        return put

    def coarsen_beta(level):
        n = N[level + 1]

        def body(i, pi):
            def child(c, a, k):
                return beta[level][c, HX[level] + 2 * i + a, pl.ds(HY[level] + k, n, stride=2), :]

            even = 0.25 * ((child(0, 0, 0) + child(0, 1, 1)) + (child(1, 0, 1) + child(1, 1, 0)))
            odd = 0.25 * ((child(1, 0, 0) + child(1, 1, 1)) + (child(0, 0, 1) + child(0, 1, 0)))
            put_coarse(beta[level + 1], level + 1, i, even, odd)(pi)

        rows(0, n, body)

    def residual(level):
        n, nc = N[level], N[level + 1]
        y0, padded = lines(level, 0)

        def body(x, px, count):
            values = finish(solved(level, 0, x, count, y0, padded, black_p[level]), px)
            for j, value in enumerate(values):
                left = (value - load(red_p[level], (x + j,), y0, padded)) * load(diag[level], (x + j,), y0, padded)
                store(res, (x + j - HX[level],), 0, padded, left)
                field[level][x + j, pl.ds(y0, n)] = black_p[level][x + j, pl.ds(y0, n)]

        chunks(HX[level], n, body, GROUP)

        def restrict(i, pi):
            def child(a, k):
                return res[2 * i + a, pl.ds(k, nc, stride=2), :]

            put_coarse(b[level + 1], level + 1, i, 0.25 * (child(0, 0) + child(1, 1)), 0.25 * (child(0, 1) + child(1, 0)))(pi)

        rows(0, nc, restrict, 8)

    def prolong(level, x0, nx, y0, n, red):
        half = n // 2
        i0 = HX[level + 1] + (x0 - HX[level]) // 2
        j0 = HY[level + 1] + (y0 - HY[level]) // 2

        def body(i, pi):
            first, second = red[i, pl.ds(j0, half), :], black_p[level + 1][i, pl.ds(j0, half), :]
            swapped = odd_rows(half, j0 + pi)
            even, odd = jnp.where(swapped, second, first), jnp.where(swapped, first, second)
            for a in (0, 1):
                x = x0 + 2 * (i - i0) + a
                for k in (0, 1):
                    here = (x, pl.ds(y0 + k, half, stride=2), slice(None))
                    black_p[level][here] = field[level][here] + (odd if a == k else even)

        rows(i0, nx // 2, body, 6)

    def descend(level):
        half_sweep(level, 1, 3, norm[level], (0,))
        half_sweep(level, 0, 2)
        half_sweep(level, 1, 1)
        residual(level)

    barrier = pltpu.get_barrier_semaphore()
    for a, c in PARTNERS:
        pl.semaphore_signal(barrier, inc=1, device_id=device(a, c), device_id_type=MESH)
    fetch_inv = pltpu.make_async_copy(inv_hbm, inv_ref, load_sem.at[0])
    fetch_src = pltpu.make_async_copy(src_hbm, src_ref, load_sem.at[1])
    fetch_inv.start()
    fetch_src.start()

    wide = lax.broadcasted_iota(jnp.int32, (16, LANES), 1)

    def take(ref, to):
        def body(x, px):
            odd = odd_rows(16, px).astype(jnp.int32)
            low = wide < LANES // 2
            lower, upper = ref[x, :, pl.ds(0, LANES)], ref[x, :, pl.ds(LANES, LANES)]
            for c in (0, 1):
                slot = lax.rem(2 * wide + (odd if c == 0 else 1 - odd), LANES)
                value = jnp.where(low, jnp.take_along_axis(lower, slot, axis=1), jnp.take_along_axis(upper, slot, axis=1))
                to[c, HX[0] + x, pl.ds(HY[0], 16)] = value

        rows(0, 16, body, 8)

    fetch_inv.wait()
    take(inv_ref, beta[0])
    pl.semaphore_wait(barrier, len(PARTNERS))
    send("e0k")
    send("e0")
    fetch_src.wait()
    take(src_ref, b[0])
    send("b0")
    send("b0k")
    for level in (0, 1, 2):
        coarsen_beta(level)
    send("e1")
    send("e2")
    receive("e0k", "e0", "b0", "b0k")
    set_up(0, 4, 8)
    normalise(0, 4)
    descend(0)

    send("b1")
    receive("e1")
    set_up(1, 6, 4)
    receive("b1")
    normalise(1, 6)
    descend(1)

    send("b2")
    send("e3")
    receive("e2")
    set_up(2, 7, 6)
    receive("b2")
    normalise(2, 4)
    descend(2)

    send("b3")
    send("b2far")
    send("f2")
    receive("e3")
    set_up(3, 6, 14)
    receive("b3")
    normalise(3, 6)
    half_sweep(3, 1, 5, norm[3], (0,))
    for step in range(2, 7):
        half_sweep(3, step % 2, 6 - step)
    for x in range(HX[3], HX[3] + N[3]):
        field[3][x, pl.ds(HY[3], N[3])] = red_p[3][x, pl.ds(HY[3], N[3])]
    send("f3")
    send("f1")
    send("f0")

    def keep_rhs(x, px):
        for c in (0, 1):
            b2w[c, x, pl.ds(6, 12)] = b[2][c, x, pl.ds(6, 12)]

    rows(4, 12, keep_rhs, 6)
    for name in NAMES:
        if name not in ("f0", "f1", "f3"):
            await_bytes(send_sem, name)
    receive("b2far")
    normalise(2, 7, b2w)
    receive("f2")
    receive("f3")
    half_sweep(3, 1, 5, field[3])

    prolong(2, 0, 20, 2, 24, field[3])
    for step in range(4):
        half_sweep(2, step % 2, 7 - step)
    receive("f1")
    prolong(1, 0, 24, 2, 24, red_p[2])
    for step in range(4):
        half_sweep(1, step % 2, 6 - step)
    receive("f0")
    prolong(0, 2, 24, 2, 24, red_p[1])
    for step in range(4):
        half_sweep(0, step % 2, 3 - step)

    def give(x, px):
        red, black = red_p[0][HX[0] + x, pl.ds(HY[0], 16)], black_p[0][HX[0] + x, pl.ds(HY[0], 16)]
        is_red = (wide + odd_rows(16, px).astype(jnp.int32)) % 2 == 0
        for part in (0, 1):
            slot = wide // 2 + part * (LANES // 2)
            out_ref[x, :, pl.ds(part * LANES, LANES)] = jnp.where(
                is_red, jnp.take_along_axis(red, slot, axis=1), jnp.take_along_axis(black, slot, axis=1))

    rows(0, 16, give, 8)
    for name in ("f0", "f1", "f3"):
        await_bytes(send_sem, name)


def solution(mesh):
    gx_size, gy_size = mesh.shape["gx"], mesh.shape["gy"]

    def both(level):
        return pltpu.VMEM((2, XE[level], YE[level], LANES), jnp.float32)

    def single(level):
        return pltpu.VMEM((XE[level], YE[level], LANES), jnp.float32)

    levels = range(4)
    block = pltpu.VMEM((16, 16, 2 * LANES), jnp.float32)
    scratch = [both(level) for _ in range(3) for level in levels]
    scratch += [single(level) for _ in range(2) for level in levels]
    scratch += [pltpu.VMEM((7, 2, XE[level], YE[level], LANES), jnp.float32) for level in levels]
    scratch += [single(level) for level in range(3)] + [single(level) for level in levels]
    scratch += [both(2), pltpu.VMEM((16, 16, LANES), jnp.float32), block, block]
    scratch += [pltpu.VMEM((MOST, LANES), jnp.float32), pltpu.SemaphoreType.DMA((2,))]
    scratch += [pltpu.SemaphoreType.DMA((len(NAMES),))] * 2

    def on_device(source, inv_density):
        hbm = pl.BlockSpec(memory_space=pltpu.HBM)

        def body(*refs):
            kernel(gx_size, gy_size, *refs)

        return pl.pallas_call(
            body,
            out_shape=pltpu.VMEM(source.shape, jnp.float32),
            in_specs=[hbm, hbm],
            out_specs=pl.BlockSpec(memory_space=pltpu.VMEM),
            scratch_shapes=scratch,
            name="v_cycle",
            compiler_params=pltpu.CompilerParams(
                collective_id=0, has_side_effects=True, vmem_limit_bytes=60 << 20
            ),
        )(source, inv_density)

    placed = P("gx", "gy", None)
    return jax.shard_map(
        on_device, mesh=mesh, in_specs=(placed, placed), out_specs=placed, check_vma=False
    )
```

time: 66.8 us -> 53.4 us (0.80)
  Pallas kernels: 64 us -> 52.5 us
  local copies, waits for them, and re-layouts: 2.6 us -> 0.71 us
    pallas_call x1, Pallas kernels: 64 us -> 52.5 us  [on_device(): pl.pallas_call(body, out_shape=pltpu.VMEM(source.shape, jnp.float32), in_...]
    unnamed x5 -> x1, local copies, waits for them, and re-layouts: 2.6 us -> 0.71 us
where the time goes in v2:
time: 53.4 us; the launch traced here: 53.2 us
  Pallas kernels  52.5 us (98%)
  local copies, waits for them, and re-layouts  0.71 us (1%)
    pallas_call x1, Pallas kernels, on_device(): pl.pallas_call(body, out_shape=pltpu.VMEM(source.shape, jnp.float32), in_...  52.5 us

profile of v2, /device:TPU:1, one launch (start us, length us, event | category | flops | bytes accessed | tf_op | source)
XLA Modules:
  0.0 53.2 jit_solution(7297978062530920376)
XLA Ops:
  0.0 52.5 %v_cycle.1 = f32[16,16,256]{2,1,0:T(8,128)S(1)} custom-call(f32[16,16,256]{2,1,0:T(8,128)} %refs_0_.1, f32[16,16,256]{2,1,0:T(8,128)} %refs_1_.1), custom_call_target="tpu_custom_call" | custom-call | tf_op jit(solution)/shard_map/v_cycle/pallas_call | solution.py:437
  52.5 0.7 %copy.4 = f32[16,16,256]{2,1,0:T(8,128)} copy(f32[16,16,256]{2,1,0:T(8,128)S(1)} %v_cycle.1) | data formatting | bytes 524288

commit v3 on v2

--- a/solution.py
+++ b/solution.py
@@ -36,6 +36,18 @@
     return sorted(out, key=lambda m: (m[1] != 0, m[0] == 0))
 
 
+def along_x(n, radius):
+    return [m for m in spread(n, radius) if m[1] == 0]
+
+
+def along_y(n, radius):
+    out = []
+    for _, c, _, _, y0, ny in [m for m in spread(n, radius) if m[0] == 0]:
+        width = radius - ((abs(c) - 1) * n + 1)
+        out.append((0, c, -width, n + 2 * width, y0, ny))
+    return out
+
+
 def near(a, b):
     return max(abs(a), abs(b)) == 1
 
@@ -51,21 +63,26 @@
     "e0": (0, RED, spread(16, 4)),
     "e0k": (0, BLACK, spread(16, 5)),
     "e1": (1, BOTH, spread(8, 7)),
-    "e2": (2, BOTH, spread(4, 8)),
-    "e3": (3, BOTH, spread(2, 7)),
-    "f0": (0, ONE, spread(16, 4)),
+    "e2x": (2, BOTH, along_x(4, 8)),
+    "e2y": (2, BOTH, along_y(4, 8)),
+    "e3x": (3, BOTH, along_x(2, 7)),
+    "e3y": (3, BOTH, along_y(2, 7)),
+    "f0x": (0, ONE, along_x(16, 4)),
+    "f0y": (0, ONE, along_y(16, 4)),
     "b1": (1, BOTH, spread(8, 6)),
-    "f1": (1, ONE, spread(8, 7)),
+    "f1x": (1, ONE, along_x(8, 7)),
+    "f1y": (1, ONE, along_y(8, 7)),
     "b2": (2, BOTH, spread(4, 8, near)),
     "b2far": (2, BOTH, spread(4, 7, far)),
-    "f2": (2, ONE, spread(4, 8)),
+    "f2x": (2, ONE, along_x(4, 8)),
+    "f2y": (2, ONE, along_y(4, 8)),
     "b3": (3, BOTH, spread(2, 6)),
     "f3": (3, ONE, spread(2, 6)),
 }
 NAMES = tuple(GROUPS)
 COUNT = {k: (2 if c == BOTH else 1) * sum(m[3] * m[5] for m in msgs) for k, (_, c, msgs) in GROUPS.items()}
 MOST = -(-max(COUNT.values()) // 8) * 8
-PARTNERS = [m[:2] for m in GROUPS["e2"][2]]
+PARTNERS = [m[:2] for m in spread(1, 2, near)] + [(a, 0) for a in (-4, -3, -2, 2, 3, 4)] + [(0, -4), (0, 4)]
 
 
 def rows(x0, nx, body, group=4):
@@ -99,7 +116,9 @@
     b2w, res, src_ref, inv_ref, dummy, load_sem, send_sem, recv_sem = scratch[31:]
     sent = {"b2far": b[2], "b0k": b[0], "e0k": beta[0]}
     for level in range(4):
-        sent.update({"e%d" % level: beta[level], "b%d" % level: b[level], "f%d" % level: field[level]})
+        for end in ("", "x", "y"):
+            sent.update({"e%d%s" % (level, end): beta[level], "f%d%s" % (level, end): field[level]})
+        sent["b%d" % level] = b[level]
     landed = dict(sent, b2far=b2w)
 
     ix, iy = lax.axis_index("gx"), lax.axis_index("gy")
@@ -186,7 +205,7 @@
             for c in (0, 1):
                 store(norm[level], (c, x), y0, n, load(rhs, (c, x), y0, n) * load(coef[level], (6, c, x), y0, n))
 
-        rows(HX[level] - radius, N[level] + 2 * radius, body, 10)
+        rows(HX[level] - radius, N[level] + 2 * radius, body, 24)
 
     def solved(level, c, x0, count, y0, n, other, lead=()):
         mids = [load(other, lead + (x0 + j - 1,), y0, n) for j in range(count + 2)]
@@ -291,7 +310,7 @@
                     here = (x, pl.ds(y0 + k, half, stride=2), slice(None))
                     black_p[level][here] = field[level][here] + (odd if a == k else even)
 
-        rows(i0, nx // 2, body, 6)
+        rows(i0, nx // 2, body, 12)
 
     def descend(level):
         half_sweep(level, 1, 3, norm[level], (0,))
@@ -319,45 +338,56 @@
                 value = jnp.where(low, jnp.take_along_axis(lower, slot, axis=1), jnp.take_along_axis(upper, slot, axis=1))
                 to[c, HX[0] + x, pl.ds(HY[0], 16)] = value
 
-        rows(0, 16, body, 8)
+        rows(0, 16, body, 16)
 
     fetch_inv.wait()
     take(inv_ref, beta[0])
+    fetch_src.wait()
+    take(src_ref, b[0])
     pl.semaphore_wait(barrier, len(PARTNERS))
     send("e0k")
     send("e0")
-    fetch_src.wait()
-    take(src_ref, b[0])
     send("b0")
     send("b0k")
     for level in (0, 1, 2):
         coarsen_beta(level)
     send("e1")
-    send("e2")
-    receive("e0k", "e0", "b0", "b0k")
+    send("e2x")
+    receive("e0k", "e0")
     set_up(0, 4, 8)
+    receive("b0", "b0k")
     normalise(0, 4)
     descend(0)
 
     send("b1")
+    receive("e2x")
+    send("e2y")
+    send("e3x")
+    send("f0x")
     receive("e1")
     set_up(1, 6, 4)
     receive("b1")
+    normalise(1, 4)
+    descend(1)
+
+    send("b2")
+    receive("e3x", "f0x")
+    send("e3y")
+    send("f1x")
     normalise(1, 6)
-    descend(1)
-
-    send("b2")
-    send("e3")
-    receive("e2")
+    receive("e2y")
     set_up(2, 7, 6)
     receive("b2")
     normalise(2, 4)
     descend(2)
 
     send("b3")
+    send("f2x")
     send("b2far")
-    send("f2")
-    receive("e3")
+    receive("f1x")
+    send("f1y")
+    send("f0y")
+    receive("e3y")
     set_up(3, 6, 14)
     receive("b3")
     normalise(3, 6)
@@ -367,8 +397,8 @@
     for x in range(HX[3], HX[3] + N[3]):
         field[3][x, pl.ds(HY[3], N[3])] = red_p[3][x, pl.ds(HY[3], N[3])]
     send("f3")
-    send("f1")
-    send("f0")
+    receive("f2x")
+    send("f2y")
 
     def keep_rhs(x, px):
         for c in (0, 1):
@@ -376,22 +406,22 @@
 
     rows(4, 12, keep_rhs, 6)
     for name in NAMES:
-        if name not in ("f0", "f1", "f3"):
+        if name not in ("f2y", "f3"):
             await_bytes(send_sem, name)
     receive("b2far")
     normalise(2, 7, b2w)
-    receive("f2")
     receive("f3")
     half_sweep(3, 1, 5, field[3])
 
+    receive("f2y")
     prolong(2, 0, 20, 2, 24, field[3])
     for step in range(4):
         half_sweep(2, step % 2, 7 - step)
-    receive("f1")
+    receive("f1y")
     prolong(1, 0, 24, 2, 24, red_p[2])
     for step in range(4):
         half_sweep(1, step % 2, 6 - step)
-    receive("f0")
+    receive("f0y")
     prolong(0, 2, 24, 2, 24, red_p[1])
     for step in range(4):
         half_sweep(0, step % 2, 3 - step)
@@ -404,8 +434,8 @@
             out_ref[x, :, pl.ds(part * LANES, LANES)] = jnp.where(
                 is_red, jnp.take_along_axis(red, slot, axis=1), jnp.take_along_axis(black, slot, axis=1))
 
-    rows(0, 16, give, 8)
-    for name in ("f0", "f1", "f3"):
+    rows(0, 16, give, 16)
+    for name in ("f2y", "f3"):
         await_bytes(send_sem, name)
 
 

time: 53.4 us -> 51 us (0.955)
  Pallas kernels: 52.5 us -> 50.1 us
    pallas_call x1, Pallas kernels: 52.5 us -> 50.1 us  [on_device(): pl.pallas_call(body, out_shape=pltpu.VMEM(source.shape, jnp.float32), in_...]
where the time goes in v3:
time: 51 us; the launch traced here: 50.8 us
  Pallas kernels  50.1 us (98%)
  local copies, waits for them, and re-layouts  0.71 us (1%)
    pallas_call x1, Pallas kernels, on_device(): pl.pallas_call(body, out_shape=pltpu.VMEM(source.shape, jnp.float32), in_...  50.1 us

profile of v3, /device:TPU:1, one launch (start us, length us, event | category | flops | bytes accessed | tf_op | source)
XLA Modules:
  0.0 50.8 jit_solution(12434736793975293450)
XLA Ops:
  0.0 50.1 %v_cycle.1 = f32[16,16,256]{2,1,0:T(8,128)S(1)} custom-call(f32[16,16,256]{2,1,0:T(8,128)} %refs_0_.1, f32[16,16,256]{2,1,0:T(8,128)} %refs_1_.1), custom_call_target="tpu_custom_call" | custom-call | tf_op jit(solution)/shard_map/v_cycle/pallas_call | solution.py:467
  50.1 0.7 %copy.4 = f32[16,16,256]{2,1,0:T(8,128)} copy(f32[16,16,256]{2,1,0:T(8,128)S(1)} %v_cycle.1) | data formatting | bytes 524288

commit v4 on v3

--- a/solution.py
+++ b/solution.py
@@ -33,6 +33,8 @@
             x0, x1 = max(-a * n, -rx), min(-a * n + n, n + rx)
             y0, y1 = max(-b * n, -ry), min(-b * n + n, n + ry)
             out.append((a, b, x0, x1 - x0, y0, y1 - y0))
+    if n == 2:
+        return sorted(out, key=lambda m: -(2 * abs(m[0]) + abs(m[1])))
     return sorted(out, key=lambda m: (m[1] != 0, m[0] == 0))
 
 
@@ -52,28 +54,28 @@
     return max(abs(a), abs(b)) == 1
 
 
-def far(a, b):
-    return max(abs(a), abs(b)) > 1
-
-
 BOTH, ONE, RED, BLACK = (slice(None),), (), (0,), (1,)
 GROUPS = {
     "b0": (0, RED, spread(16, 4)),
     "b0k": (0, BLACK, spread(16, 3)),
     "e0": (0, RED, spread(16, 4)),
     "e0k": (0, BLACK, spread(16, 5)),
-    "e1": (1, BOTH, spread(8, 7)),
+    "e1x": (1, BOTH, along_x(8, 7)),
+    "e1y": (1, BOTH, along_y(8, 7)),
     "e2x": (2, BOTH, along_x(4, 8)),
     "e2y": (2, BOTH, along_y(4, 8)),
     "e3x": (3, BOTH, along_x(2, 7)),
     "e3y": (3, BOTH, along_y(2, 7)),
     "f0x": (0, ONE, along_x(16, 4)),
     "f0y": (0, ONE, along_y(16, 4)),
-    "b1": (1, BOTH, spread(8, 6)),
+    "b1": (1, BOTH, spread(8, 4)),
+    "b1x": (1, BOTH, along_x(8, 6)),
+    "b1y": (1, BOTH, along_y(8, 6)),
     "f1x": (1, ONE, along_x(8, 7)),
     "f1y": (1, ONE, along_y(8, 7)),
-    "b2": (2, BOTH, spread(4, 8, near)),
-    "b2far": (2, BOTH, spread(4, 7, far)),
+    "b2": (2, BOTH, spread(4, 4)),
+    "b2x": (2, BOTH, along_x(4, 7)),
+    "b2y": (2, BOTH, along_y(4, 7)),
     "f2x": (2, ONE, along_x(4, 8)),
     "f2y": (2, ONE, along_y(4, 8)),
     "b3": (3, BOTH, spread(2, 6)),
@@ -113,13 +115,13 @@
 def kernel(gx_size, gy_size, src_hbm, inv_hbm, out_ref, *scratch):
     beta, b, norm, red_p, black_p, coef = (scratch[4 * k : 4 * k + 4] for k in range(6))
     diag, field = scratch[24:27], scratch[27:31]
-    b2w, res, src_ref, inv_ref, dummy, load_sem, send_sem, recv_sem = scratch[31:]
-    sent = {"b2far": b[2], "b0k": b[0], "e0k": beta[0]}
+    b1w, b2w, res, src_ref, inv_ref, dummy, load_sem, send_sem, recv_sem = scratch[31:]
+    sent = {"b1x": b[1], "b1y": b1w, "b2x": b[2], "b2y": b2w, "b0k": b[0], "e0k": beta[0]}
     for level in range(4):
         for end in ("", "x", "y"):
             sent.update({"e%d%s" % (level, end): beta[level], "f%d%s" % (level, end): field[level]})
         sent["b%d" % level] = b[level]
-    landed = dict(sent, b2far=b2w)
+    landed = dict(sent, b1x=b1w, b2x=b2w)
 
     ix, iy = lax.axis_index("gx"), lax.axis_index("gy")
     at_x = {a: lax.rem(ix + (a + gx_size), gx_size) for a in range(-4, 5)}
@@ -312,6 +314,14 @@
 
         rows(i0, nx // 2, body, 12)
 
+    def keep_own(level, to):
+        def body(x, px):
+            for c in (0, 1):
+                here = (c, HX[level] + x, pl.ds(HY[level], N[level]))
+                to[here] = b[level][here]
+
+        rows(0, N[level], body, 8)
+
     def descend(level):
         half_sweep(level, 1, 3, norm[level], (0,))
         half_sweep(level, 0, 2)
@@ -319,12 +329,12 @@
         residual(level)
 
     barrier = pltpu.get_barrier_semaphore()
-    for a, c in PARTNERS:
-        pl.semaphore_signal(barrier, inc=1, device_id=device(a, c), device_id_type=MESH)
     fetch_inv = pltpu.make_async_copy(inv_hbm, inv_ref, load_sem.at[0])
     fetch_src = pltpu.make_async_copy(src_hbm, src_ref, load_sem.at[1])
     fetch_inv.start()
     fetch_src.start()
+    for a, c in PARTNERS:
+        pl.semaphore_signal(barrier, inc=1, device_id=device(a, c), device_id_type=MESH)
 
     wide = lax.broadcasted_iota(jnp.int32, (16, LANES), 1)
 
@@ -351,7 +361,7 @@
     send("b0k")
     for level in (0, 1, 2):
         coarsen_beta(level)
-    send("e1")
+    send("e1x")
     send("e2x")
     receive("e0k", "e0")
     set_up(0, 4, 8)
@@ -360,21 +370,25 @@
     descend(0)
 
     send("b1")
-    receive("e2x")
+    receive("e1x", "e2x")
+    send("e1y")
     send("e2y")
+    send("b1x")
     send("e3x")
     send("f0x")
-    receive("e1")
+    keep_own(1, b1w)
+    receive("e1y")
     set_up(1, 6, 4)
     receive("b1")
     normalise(1, 4)
     descend(1)
 
     send("b2")
-    receive("e3x", "f0x")
+    receive("e3x", "f0x", "b1x")
     send("e3y")
     send("f1x")
-    normalise(1, 6)
+    send("b1y")
+    keep_own(2, b2w)
     receive("e2y")
     set_up(2, 7, 6)
     receive("b2")
@@ -383,7 +397,7 @@
 
     send("b3")
     send("f2x")
-    send("b2far")
+    send("b2x")
     receive("f1x")
     send("f1y")
     send("f0y")
@@ -397,18 +411,16 @@
     for x in range(HX[3], HX[3] + N[3]):
         field[3][x, pl.ds(HY[3], N[3])] = red_p[3][x, pl.ds(HY[3], N[3])]
     send("f3")
-    receive("f2x")
+    receive("f2x", "b2x")
     send("f2y")
-
-    def keep_rhs(x, px):
-        for c in (0, 1):
-            b2w[c, x, pl.ds(6, 12)] = b[2][c, x, pl.ds(6, 12)]
-
-    rows(4, 12, keep_rhs, 6)
+    send("b2y")
+
     for name in NAMES:
-        if name not in ("f2y", "f3"):
+        if name not in ("b2y", "f2y", "f3"):
             await_bytes(send_sem, name)
-    receive("b2far")
+    receive("b1y")
+    normalise(1, 6, b1w)
+    receive("b2y")
     normalise(2, 7, b2w)
     receive("f3")
     half_sweep(3, 1, 5, field[3])
@@ -435,7 +447,7 @@
                 is_red, jnp.take_along_axis(red, slot, axis=1), jnp.take_along_axis(black, slot, axis=1))
 
     rows(0, 16, give, 16)
-    for name in ("f2y", "f3"):
+    for name in ("b2y", "f2y", "f3"):
         await_bytes(send_sem, name)
 
 
@@ -454,7 +466,7 @@
     scratch += [single(level) for _ in range(2) for level in levels]
     scratch += [pltpu.VMEM((7, 2, XE[level], YE[level], LANES), jnp.float32) for level in levels]
     scratch += [single(level) for level in range(3)] + [single(level) for level in levels]
-    scratch += [both(2), pltpu.VMEM((16, 16, LANES), jnp.float32), block, block]
+    scratch += [both(1), both(2), pltpu.VMEM((16, 16, LANES), jnp.float32), block, block]
     scratch += [pltpu.VMEM((MOST, LANES), jnp.float32), pltpu.SemaphoreType.DMA((2,))]
     scratch += [pltpu.SemaphoreType.DMA((len(NAMES),))] * 2
 

time: 51 us -> 49.5 us (0.971)
  Pallas kernels: 50.1 us -> 48.7 us
    pallas_call x1, Pallas kernels: 50.1 us -> 48.7 us  [on_device(): pl.pallas_call(body, out_shape=pltpu.VMEM(source.shape, jnp.float32), in_...]
where the time goes in v4:
time: 49.5 us; the launch traced here: 49.4 us
  Pallas kernels  48.7 us (98%)
  local copies, waits for them, and re-layouts  0.71 us (1%)
    pallas_call x1, Pallas kernels, on_device(): pl.pallas_call(body, out_shape=pltpu.VMEM(source.shape, jnp.float32), in_...  48.7 us

profile of v4, /device:TPU:1, one launch (start us, length us, event | category | flops | bytes accessed | tf_op | source)
XLA Modules:
  0.0 49.4 jit_solution(5708790592554826793)
XLA Ops:
  0.0 48.7 %v_cycle.1 = f32[16,16,256]{2,1,0:T(8,128)S(1)} custom-call(f32[16,16,256]{2,1,0:T(8,128)} %refs_0_.1, f32[16,16,256]{2,1,0:T(8,128)} %refs_1_.1), custom_call_target="tpu_custom_call" | custom-call | tf_op jit(solution)/shard_map/v_cycle/pallas_call | solution.py:479
  48.7 0.7 %copy.4 = f32[16,16,256]{2,1,0:T(8,128)} copy(f32[16,16,256]{2,1,0:T(8,128)S(1)} %v_cycle.1) | data formatting | bytes 524288

commit v5 on v4

--- a/solution.py
+++ b/solution.py
@@ -378,7 +378,7 @@
     send("f0x")
     keep_own(1, b1w)
     receive("e1y")
-    set_up(1, 6, 4)
+    set_up(1, 4, 8)
     receive("b1")
     normalise(1, 4)
     descend(1)
@@ -390,7 +390,7 @@
     send("b1y")
     keep_own(2, b2w)
     receive("e2y")
-    set_up(2, 7, 6)
+    set_up(2, 4, 6)
     receive("b2")
     normalise(2, 4)
     descend(2)
@@ -418,6 +418,8 @@
     for name in NAMES:
         if name not in ("b2y", "f2y", "f3"):
             await_bytes(send_sem, name)
+    set_up(1, 6, 4)
+    set_up(2, 7, 6)
     receive("b1y")
     normalise(1, 6, b1w)
     receive("b2y")

time: 49.5 us -> 49.3 us (level)
  no operation moved by 1% of the time
where the time goes in v5:
time: 49.3 us; the launch traced here: 49.2 us
  Pallas kernels  48.5 us (98%)
  local copies, waits for them, and re-layouts  0.71 us (1%)
    pallas_call x1, Pallas kernels, on_device(): pl.pallas_call(body, out_shape=pltpu.VMEM(source.shape, jnp.float32), in_...  48.5 us

profile of v5, /device:TPU:1, one launch (start us, length us, event | category | flops | bytes accessed | tf_op | source)
XLA Modules:
  0.0 49.2 jit_solution(14819258104571613781)
XLA Ops:
  0.0 48.5 %v_cycle.1 = f32[16,16,256]{2,1,0:T(8,128)S(1)} custom-call(f32[16,16,256]{2,1,0:T(8,128)} %refs_0_.1, f32[16,16,256]{2,1,0:T(8,128)} %refs_1_.1), custom_call_target="tpu_custom_call" | custom-call | tf_op jit(solution)/shard_map/v_cycle/pallas_call | solution.py:481
  48.5 0.7 %copy.4 = f32[16,16,256]{2,1,0:T(8,128)} copy(f32[16,16,256]{2,1,0:T(8,128)S(1)} %v_cycle.1) | data formatting | bytes 524288
